TPU v7x, 32 devices: a whole 2x2x4 slice. The times are simulated.
32 devices in a mesh: groups: 2 (over x), ctx: 16 (over z, y, core).
Axes of the slice: x: 2, y: 2, z: 4, core: 2. Of those that a mesh axis runs over, the one named last changes fastest.
Arguments:
- states: bfloat16 [4096, 3072], P(('groups', 'ctx')), parts along dimension 0, may hold values from -6 to 6
- queries: bfloat16 [4096, 3072], P(('groups', 'ctx')), parts along dimension 0, may hold values from -256 to 256
- keys: bfloat16 [4096, 512], P(('groups', 'ctx')), parts along dimension 0, may hold values from -8 to 8
- values: bfloat16 [4096, 512], P(('groups', 'ctx')), parts along dimension 0, may hold values from -6 to 6
- norm_gain: float32 [3072], replicated, may hold values from 0.5 to 1.5
- router: bfloat16 [3072, 8], replicated, may hold values from -0.109375 to 0.109375
- routes: int32 [4096, 1], P(('groups', 'ctx')), parts along dimension 0, may hold values from 0 to 7; in each aligned block of 128 rows (0 to 127, 128 to 255, ...) at most 18 rows name the same one
- w_gate: bfloat16 [16384, 3072], P('ctx'), may hold values from -0.109375 to 0.109375
- w_up: bfloat16 [16384, 3072], P('ctx'), may hold values from -0.109375 to 0.109375
- w_down: bfloat16 [16384, 3072], P('ctx'), may hold values from -0.0625 to 0.0625
Outputs:
- attended: bfloat16 [4096, 3072], P(('groups', 'ctx')), parts along dimension 0
- mixed_states: bfloat16 [4096, 3072], P(('groups', 'ctx')), parts along dimension 0
There are 2 independent parts, one for each index of `groups`. A program takes and returns all parts, laid end to end along the dimension named above; an argument that names none is the same for every part. Nothing has to cross between parts.
Inputs may be any that keep to these rules, and one draw needn't show every extreme that they name: `routes`: among the rows of one device no expert is named by more than 18 rows, and in every draw some expert is named by exactly 18 rows of some device.
All inputs are finite; a program needn't handle non-finite values.
Results may differ from a plain program's by a relative error of at most 0.004.
Values may be sent and summed in bfloat16 or wider, within the bound.
A program may use at most 320 MiB of HBM per device.

v0:
```python
import math

import jax
import jax.numpy as jnp
from jax import lax
from jax.sharding import PartitionSpec as P

HD = 128
E = 2
CAP = 18


def expert_slice(rows, gate_rows, up_rows, down_rows):
    dims = (((1,), (1,)), ((), ()))
    gated = lax.dot_general(rows, gate_rows, dims, preferred_element_type=jnp.float32)
    upward = lax.dot_general(rows, up_rows, dims, preferred_element_type=jnp.float32)
    hidden = (jax.nn.silu(gated) * upward).astype(jnp.bfloat16)
    return jnp.dot(hidden, down_rows, preferred_element_type=jnp.float32)


def normalize(states, norm_gain):
    wide = states.astype(jnp.float32)
    meansq = jnp.mean(wide * wide, axis=-1, keepdims=True)
    return (wide * lax.rsqrt(meansq + 1e-05) * norm_gain).astype(jnp.bfloat16)


def body(states, queries, keys, values, norm_gain, router, routes, w_gate, w_up, w_down):
    local_rows = states.shape[0]
    width = states.shape[1]
    query_width = queries.shape[1]
    kv_heads = keys.shape[1] // HD
    group = query_width // HD // kv_heads
    query_grid = queries.reshape(local_rows, kv_heads, group, HD)
    query_positions = lax.axis_index("ctx") * local_rows + jnp.arange(local_rows, dtype=jnp.int32)
    last_query = query_positions[local_rows - 1]

    def fold_block(running, shard_piece):
        old_max, old_sum, accum = running
        key_piece, value_piece = shard_piece
        piece_rows = key_piece.shape[0]
        key_grid = key_piece.reshape(piece_rows, kv_heads, HD)
        value_grid = value_piece.reshape(piece_rows, kv_heads, HD)
        scores = jnp.einsum(
            "qhgd,khd->hgqk", query_grid, key_grid, preferred_element_type=jnp.float32
        ) / math.sqrt(HD)
        key_positions = jnp.arange(piece_rows, dtype=jnp.int32)
        visible = key_positions[None, :] <= query_positions[:, None]
        scores = jnp.where(visible, scores, -1e30)
        new_max = jnp.maximum(old_max, jnp.max(scores, axis=-1))
        expo = jnp.where(visible, jnp.exp(scores - new_max[..., None]), 0.0)
        new_sum = jnp.sum(expo, axis=-1)
        weighted = jnp.einsum(
            "hgqk,khd->hgqd",
            expo.astype(jnp.bfloat16),
            value_grid,
            preferred_element_type=jnp.float32,
        )
        return (new_max, new_sum, weighted)

    normed = normalize(states, norm_gain)
    logits = jnp.dot(normed, router, preferred_element_type=jnp.float32)
    picked = jnp.take_along_axis(logits, routes, axis=1)[:, 0]
    mixing = jax.nn.sigmoid(picked)
    devices = lax.axis_size("ctx")
    spread = devices // E
    chosen = routes[:, 0]
    in_window = chosen < E
    experts_range = jnp.arange(E, dtype=jnp.int32)
    member = (chosen[:, None] == experts_range[None, :]).astype(jnp.int32)
    ranks = jnp.sum((jnp.cumsum(member, axis=0) - member) * member, axis=1)
    slot = jnp.where(in_window, chosen * CAP + ranks, 0)
    place = (slot[None, :] == jnp.arange(E * CAP, dtype=jnp.int32)[:, None]) & in_window[None, :]
    buffer = jnp.dot(place.astype(jnp.bfloat16), normed, preferred_element_type=jnp.float32).astype(
        jnp.bfloat16
    )
    filled = jnp.sum(place.astype(jnp.int32), axis=1)
    send_rows = jnp.broadcast_to(buffer.reshape(E, 1, CAP, width), (E, spread, CAP, width)).reshape(
        devices, CAP, width
    )
    send_flags = jnp.broadcast_to(filled.reshape(E, 1, CAP), (E, spread, CAP)).reshape(devices, CAP)
    start_max = jnp.full((kv_heads, group, local_rows), -1e30, jnp.float32)
    start_sum = jnp.zeros((kv_heads, group, local_rows), jnp.float32)
    start_acc = jnp.zeros((kv_heads, group, local_rows, HD), jnp.float32)
    running = (start_max, start_sum, start_acc)
    shard_piece = (
        lax.all_gather(keys, "ctx", axis=0, tiled=True),
        lax.all_gather(values, "ctx", axis=0, tiled=True),
    )
    final_max, final_sum, final_acc = lax.cond(
        jnp.int32(0) > last_query, lambda: running, lambda: fold_block(running, shard_piece)
    )
    result = final_acc / final_sum[..., None]
    attended = result.transpose(2, 0, 1, 3).reshape(local_rows, query_width).astype(jnp.bfloat16)
    rows_in = lax.all_to_all(send_rows, "ctx", split_axis=0, concat_axis=0, tiled=True)
    flags_in = lax.all_to_all(send_flags, "ctx", split_axis=0, concat_axis=0, tiled=True)
    sources = flags_in.shape[0]
    items = flags_in.shape[1]
    total = sources * items
    flat_rows = rows_in.reshape(total, width)
    flat_flags = flags_in.reshape(total)
    before = jnp.cumsum(flat_flags) - flat_flags
    target = jnp.where(flat_flags > 0, before, total)
    order = (
        jnp.full((total + 128,), total, jnp.int32)
        .at[target]
        .set(jnp.arange(total, dtype=jnp.int32))
    )
    count = jnp.sum(flat_flags)
    used_blocks = (count + 127) // 128

    def run_block(block_index, written):
        first_slot = block_index * 128
        picked_slots = lax.dynamic_slice_in_dim(order, first_slot, 128)
        rows = jnp.take(flat_rows, jnp.minimum(picked_slots, total - 1), axis=0)
        result = expert_slice(rows, w_gate, w_up, w_down).astype(jnp.bfloat16)
        positions = first_slot + jnp.arange(128, dtype=jnp.int32)
        dest = jnp.where(positions < count, picked_slots, total)
        return written.at[dest].set(result)

    written = lax.fori_loop(0, used_blocks, run_block, jnp.zeros((total + 1, width), jnp.bfloat16))
    partial_value = written[:total].reshape(sources, items, width)
    returned = partial_value
    returned = lax.all_to_all(returned, "ctx", split_axis=0, concat_axis=0, tiled=True)
    summed = jnp.sum(returned.reshape(E, spread, CAP, width).astype(jnp.float32), axis=1).reshape(
        E * CAP, width
    )
    token_sums = jnp.where(in_window[:, None], jnp.take(summed, slot, axis=0), 0.0)
    mixed = (states.astype(jnp.float32) + mixing[:, None] * token_sums).astype(jnp.bfloat16)
    return (attended, mixed)


def solution(mesh):
    in_specs = (
        P(("groups", "ctx"), None),
        P(("groups", "ctx"), None),
        P(("groups", "ctx"), None),
        P(("groups", "ctx"), None),
        P(),
        P(),
        P(("groups", "ctx"), None),
        P("ctx", None),
        P("ctx", None),
        P("ctx", None),
    )
    out_specs = (P(("groups", "ctx"), None), P(("groups", "ctx"), None))
    return jax.shard_map(body, mesh=mesh, in_specs=in_specs, out_specs=out_specs, check_vma=False)
```

profile of v0, /device:TPU:13, one launch (start us, length us, event | category | flops | bytes accessed | tf_op | source)
XLA Modules:
  0.0 232.7 jit_solution(12496014209454178715)
XLA Ops:
  7.2 0.7 all-gather.3.cloned.1.call-update
  7.9 0.7 fusion.31
  8.8 0.8 select_reduce_fusion
  9.7 0.7 broadcast_compare_fusion
  10.3 0.7 add_select_fusion
  11.8 6.6 %all-to-all-start = ((s32[16,1,18]{2,1,0:T(1,128)}), s32[16,1,18]{2,1,0:T(1,128)S(1)}, u32[]{:S(2)}, u32[]{:S(2)}) async-start(s32[16,1,18]{2,1,0:T(1,128)} %bitcast.16), calls=%async_computation | async-start | bytes 16384 | tf_op jit(solution)/shard_map/all_to_all | solution.py:95
  18.4 1.4 fusion.24
  19.8 1.6 convolution_convert_fusion.1
  21.4 0.8 all-to-all-done
  22.2 1.7 broadcast_in_dim.123
  23.9 6.2 %all-to-all-start.1 = ((bf16[16,18,3072]{2,1,0:T(8,128)(2,1)}), bf16[16,18,3072]{2,1,0:T(8,128)(2,1)S(1)}, u32[]{:S(2)}, u32[]{:S(2)}) async-start(bf16[16,18,3072]{2,1,0:T(8,128)(2,1)} %bitcast.63), calls=%async_computation.1 | async-start | bytes 4718592 | tf_op jit(solution)/shard_map/all_to_all | solution.py:94
  30.1 0.7 all-gather.5.cloned.1.call-update
  31.4 1.3 fusion.39
  34.0 2.9 %scatter_custom_fusion.1 = s32[416]{0:T(512)S(1)} fusion(s32[288]{0:T(512)S(1)} %compare_select_fusion.3, s32[288]{0:T(512)S(1)} %iota.22, s32[]{:T(128)} %constant.123.clone.1), kind=kCustom, calls=%fused_computation.70 | custom fusion | bytes 1668 | tf_op jit(solution)/shard_map/scatter | solution.py:106
  36.9 58.9 %all-to-all-done.1 = bf16[16,18,3072]{2,1,0:T(8,128)(2,1)S(1)} async-done(((bf16[16,18,3072]{2,1,0:T(8,128)(2,1)}), bf16[16,18,3072]{2,1,0:T(8,128)(2,1)S(1)}, u32[]{:S(2)}, u32[]{:S(2)}) %all-to-all-start.1) | async-done | bytes 1769504 | tf_op jit(solution)/shard_map/all_to_all | solution.py:94
  95.8 1.5 reshape.124
  97.5 62.1 %while.10 = (s32[]{:T(128)}, bf16[289,3072]{1,0:T(8,128)(2,1)S(1)}, s32[]{:T(128)}, s32[]{:T(128)}, s32[416]{0:T(512)S(1)}, /*index=5*/bf16[288,3072]{1,0:T(8,12...) while((s32[]{:T(128)}, bf16[289,3072]{1,0:T(8,128)(2,1)S(1)}, ...), condition=%wide.region_14.15_spmd, body=%wide.region_12.14_spmd.sunk | while | flops 2417887744 | bytes 26222660 | solution.py:120
  97.5 0.6 compare_select_fusion.10
  98.2 3.5 %gather_fusion = bf16[128,3072]{1,0:T(8,128)(2,1)S(1)} fusion(bf16[288,3072]{1,0:T(8,128)(2,1)} %get-tuple-element.211, s32[1024]{0:T(1024)S(1)} %pad_clamp_fusion.3), kind=kCustom, calls=%fused_computation.clone.1 | custom fusion | bytes 1573376 | tf_op jit(solution)/shard_map/while/body/jit(_take)/gather | solution.py:114
  101.8 5.8 %fusion.52 = f32[128,1024]{1,0:T(8,128)} fusion(bf16[1024,3072]{1,0:T(8,128)(2,1)} %get-tuple-element.212, bf16[128,3072]{1,0:T(8,128)(2,1)S(1)} %gather_fusion, pred[128]{0:T(512)(128)(4,1)S(1)} %get-tuple-element.175), kind=kOutput, calls=%fused_computation.29.clone.1 | convolution fusion | flops 805699584 | bytes 7602304 | tf_op jit(solution)/shard_map/while/body/dot_general | solution.py:15
  107.6 8.0 %convolution_convert_fusion.3 = bf16[128,3072]{1,0:T(8,128)(2,1)S(1)} fusion(bf16[1024,3072]{1,0:T(8,128)(2,1)} %get-tuple-element.214, bf16[1024,3072]{1,0:T(8,128)(2,1)} %get-tuple-element.213, f32[128,1024]{1,0:T(8,128)} %fusion.52, bf16[128,3072]{1,0:T(8,128)(2,1)S(1)} %gather_fusion, pred[128]{0:T(512)(128)(4,1)S(1)} %get-tuple-element.175), kind=kOutput, calls=%fused_computation.20.clone.1 | convolution fusion | flops 1612185600 | bytes 14680192 | tf_op jit(solution)/shard_map/while/body/dot_general | solution.py:18
  115.6 2.6 %scatter_fusion = bf16[289,3072]{1,0:T(8,128)(2,1)S(1)} fusion(bf16[289,3072]{1,0:T(8,128)(2,1)S(1)} %get-tuple-element.194, s32[128]{0:T(128)S(1)} %compare_select_fusion.10, bf16[128,3072]{1,0:T(8,128)(2,1)S(1)} %convolution_convert_fusion.3), kind=kCustom, calls=%fused_computation.3.clone.1 | custom fusion | bytes 2359808 | tf_op jit(solution)/shard_map/while/body/scatter | solution.py:118
  118.2 0.6 compare_select_fusion.10
  119.0 3.5 %gather_fusion = bf16[128,3072]{1,0:T(8,128)(2,1)S(1)} fusion(bf16[288,3072]{1,0:T(8,128)(2,1)} %get-tuple-element.211, s32[1024]{0:T(1024)S(1)} %pad_clamp_fusion.3), kind=kCustom, calls=%fused_computation.clone.1 | custom fusion | bytes 1573376 | tf_op jit(solution)/shard_map/while/body/jit(_take)/gather | solution.py:114
  122.5 5.8 %fusion.52 = f32[128,1024]{1,0:T(8,128)} fusion(bf16[1024,3072]{1,0:T(8,128)(2,1)} %get-tuple-element.212, bf16[128,3072]{1,0:T(8,128)(2,1)S(1)} %gather_fusion, pred[128]{0:T(512)(128)(4,1)S(1)} %get-tuple-element.175), kind=kOutput, calls=%fused_computation.29.clone.1 | convolution fusion | flops 805699584 | bytes 7602304 | tf_op jit(solution)/shard_map/while/body/dot_general | solution.py:15
  128.3 7.9 %convolution_convert_fusion.3 = bf16[128,3072]{1,0:T(8,128)(2,1)S(1)} fusion(bf16[1024,3072]{1,0:T(8,128)(2,1)} %get-tuple-element.214, bf16[1024,3072]{1,0:T(8,128)(2,1)} %get-tuple-element.213, f32[128,1024]{1,0:T(8,128)} %fusion.52, bf16[128,3072]{1,0:T(8,128)(2,1)S(1)} %gather_fusion, pred[128]{0:T(512)(128)(4,1)S(1)} %get-tuple-element.175), kind=kOutput, calls=%fused_computation.20.clone.1 | convolution fusion | flops 1612185600 | bytes 14680192 | tf_op jit(solution)/shard_map/while/body/dot_general | solution.py:18
  136.2 2.6 %scatter_fusion = bf16[289,3072]{1,0:T(8,128)(2,1)S(1)} fusion(bf16[289,3072]{1,0:T(8,128)(2,1)S(1)} %get-tuple-element.194, s32[128]{0:T(128)S(1)} %compare_select_fusion.10, bf16[128,3072]{1,0:T(8,128)(2,1)S(1)} %convolution_convert_fusion.3), kind=kCustom, calls=%fused_computation.3.clone.1 | custom fusion | bytes 2359808 | tf_op jit(solution)/shard_map/while/body/scatter | solution.py:118
  139.6 3.5 %gather_fusion = bf16[128,3072]{1,0:T(8,128)(2,1)S(1)} fusion(bf16[288,3072]{1,0:T(8,128)(2,1)} %get-tuple-element.211, s32[1024]{0:T(1024)S(1)} %pad_clamp_fusion.3), kind=kCustom, calls=%fused_computation.clone.1 | custom fusion | bytes 1573376 | tf_op jit(solution)/shard_map/while/body/jit(_take)/gather | solution.py:114
  143.1 5.8 %fusion.52 = f32[128,1024]{1,0:T(8,128)} fusion(bf16[1024,3072]{1,0:T(8,128)(2,1)} %get-tuple-element.212, bf16[128,3072]{1,0:T(8,128)(2,1)S(1)} %gather_fusion, pred[128]{0:T(512)(128)(4,1)S(1)} %get-tuple-element.175), kind=kOutput, calls=%fused_computation.29.clone.1 | convolution fusion | flops 805699584 | bytes 7602304 | tf_op jit(solution)/shard_map/while/body/dot_general | solution.py:15
  148.9 7.9 %convolution_convert_fusion.3 = bf16[128,3072]{1,0:T(8,128)(2,1)S(1)} fusion(bf16[1024,3072]{1,0:T(8,128)(2,1)} %get-tuple-element.214, bf16[1024,3072]{1,0:T(8,128)(2,1)} %get-tuple-element.213, f32[128,1024]{1,0:T(8,128)} %fusion.52, bf16[128,3072]{1,0:T(8,128)(2,1)S(1)} %gather_fusion, pred[128]{0:T(512)(128)(4,1)S(1)} %get-tuple-element.175), kind=kOutput, calls=%fused_computation.20.clone.1 | convolution fusion | flops 1612185600 | bytes 14680192 | tf_op jit(solution)/shard_map/while/body/dot_general | solution.py:18
  156.8 2.6 %scatter_fusion = bf16[289,3072]{1,0:T(8,128)(2,1)S(1)} fusion(bf16[289,3072]{1,0:T(8,128)(2,1)S(1)} %get-tuple-element.194, s32[128]{0:T(128)S(1)} %compare_select_fusion.10, bf16[128,3072]{1,0:T(8,128)(2,1)S(1)} %convolution_convert_fusion.3), kind=kCustom, calls=%fused_computation.3.clone.1 | custom fusion | bytes 2359808 | tf_op jit(solution)/shard_map/while/body/scatter | solution.py:118
  159.6 1.3 slice.20
  160.9 2.9 %reshape.125 = bf16[16,18,3072]{2,1,0:T(8,128)(2,1)} reshape(bf16[288,3072]{1,0:T(8,128)(2,1)} %slice.20) | data formatting | bytes 3538944 | tf_op jit(solution)/shard_map/reshape | solution.py:121
  163.8 4.5 %all-to-all-start.2 = ((bf16[16,18,3072]{2,1,0:T(8,128)(2,1)}), bf16[16,18,3072]{2,1,0:T(8,128)(2,1)}, u32[]{:S(2)}, u32[]{:S(2)}) async-start(bf16[16,18,3072]{2,1,0:T(8,128)(2,1)} %reshape.125), calls=%async_computation.2 | async-start | bytes 4718592 | tf_op jit(solution)/shard_map/all_to_all | solution.py:123
  170.1 1.0 gather_fusion.2
  171.2 32.9 %conditional.1 = (f32[4,6,128]{2,1,0:T(8,128)S(1)}, f32[4,6,128,128]{2,3,1,0:T(8,128)S(1)}) conditional(s32[]{:T(128)} %bitcast.4, (s32[128]{0:T(128)S(1)}, bf16[2048,512]{1,0:T(8,128)(2,1)}, bf16[128,3072]{1,0:T(8,128)(2,1)S(1)}, bf16[2048,512]{1,0:T(8,128)(2,1)}) %tuple.56, () %tuple.21), branch_computations={%region_0.3_spmd, %region_3.4_spmd} | conditional | flops 3303273472 | bytes 193798704 | solution.py:89
  171.4 1.2 copy.36
  172.5 4.0 %reshape.108 = bf16[2048,4,128]{2,1,0:T(4,128)(2,1)} reshape(bf16[2048,512]{1,0:T(8,128)(2,1)} %get-tuple-element.46) | data formatting | bytes 4194304 | tf_op jit(solution)/shard_map/cond/branch_0_fun/reshape | solution.py:41
  176.5 5.5 %fusion = (f32[4,6,128]{2,1,0:T(8,128)S(1)}, f32[4,2048,128,6]{2,1,3,0:T(8,128)S(1)}) fusion(pred[128,2048]{0,1:T(8,128)(4,1)S(1)} %iota_compare_fusion, bf16[128,4,6,128]{0,3,2,1:T(8,128)(2,1)} %bitcast.66, bf16[2048,4,128,1]{2,1,0,3:T(4,128)(2,1)} %bitcast.64), kind=kOutput, calls=%fused_computation.7 | convolution fusion | flops 1629484032 | bytes 28323840 | tf_op jit(solution)/shard_map/cond/branch_0_fun/qhgd,khd->hgqk/dot_general | solution.py:43
  182.0 6.1 %fusion.2 = f32[4,6,128]{2,1,0:T(8,128)S(1)} fusion(f32[4,2048,128,6]{2,1,3,0:T(8,128)S(1)} %get-tuple-element.114, f32[4,6,128]{2,1,0:T(8,128)S(1)} %broadcast_maximum_fusion, pred[128,2048]{0,1:T(8,128)(4,1)S(1)} %iota_compare_fusion), kind=kLoop, calls=%fused_computation.9 | loop fusion | flops 31454208 | bytes 25452544 | tf_op jit(solution)/shard_map/cond/branch_0_fun/reduce_sum | solution.py:51
  188.1 2.2 copy-done.1
  190.3 2.5 %reshape.110 = bf16[2048,4,128]{2,1,0:T(4,128)(2,1)S(1)} reshape(bf16[2048,512]{1,0:T(8,128)(2,1)} %get-tuple-element.48) | data formatting | bytes 4194304 | tf_op jit(solution)/shard_map/cond/branch_0_fun/reshape | solution.py:42
  192.9 11.2 %fusion.3 = f32[4,6,128,128]{2,3,1,0:T(8,128)S(1)} fusion(f32[4,2048,128,6]{2,1,3,0:T(8,128)} %copy-done.1, f32[4,6,128]{2,1,0:T(8,128)S(1)} %broadcast_maximum_fusion, pred[128,2048]{0,1:T(8,128)(4,1)S(1)} %iota_compare_fusion, bf16[2048,4,128,1]{2,1,0,3:T(4,128)(2,1)S(1)} %bitcast.67), kind=kOutput, calls=%fused_computation.10 | convolution fusion | flops 1642070016 | bytes 29110272 | tf_op jit(solution)/shard_map/cond | solution.py:89
  204.3 1.2 copy.38
  205.5 15.7 %all-to-all-done.2 = bf16[16,18,3072]{2,1,0:T(8,128)(2,1)} async-done(((bf16[16,18,3072]{2,1,0:T(8,128)(2,1)}), bf16[16,18,3072]{2,1,0:T(8,128)(2,1)}, u32[]{:S(2)}, u32[]{:S(2)}) %all-to-all-start.2) | async-done | bytes 1769504 | tf_op jit(solution)/shard_map/all_to_all | solution.py:123
  221.2 2.1 convert_reduce_fusion
  223.3 1.2 gather_fusion.1
  224.5 1.3 fusion.27
  (55 shorter events, 5.0 us)
Async XLA Ops:
  7.2 162.5 %copy-start = (bf16[3072,8]{0,1:T(8,128)(2,1)S(1)}, bf16[3072,8]{0,1:T(8,128)(2,1)}, u32[]{:S(2)}) copy-start(bf16[3072,8]{0,1:T(8,128)(2,1)} %param.19) | copy-start | bytes 147460
  7.2 164.0 %all-gather.3.cloned.1.call-start = ((), (), s32[]{:S(2)}) async-start(), calls=%async_computation.3 | async-start | bytes 2228224 | tf_op jit(solution)/shard_map/all_gather | solution.py:86
  11.8 10.4 %all-to-all-start = ((s32[16,1,18]{2,1,0:T(1,128)}), s32[16,1,18]{2,1,0:T(1,128)S(1)}, u32[]{:S(2)}, u32[]{:S(2)}) async-start(s32[16,1,18]{2,1,0:T(1,128)} %bitcast.16), calls=%async_computation | async-start | bytes 16384 | tf_op jit(solution)/shard_map/all_to_all | solution.py:95
  23.9 71.9 %all-to-all-start.1 = ((bf16[16,18,3072]{2,1,0:T(8,128)(2,1)}), bf16[16,18,3072]{2,1,0:T(8,128)(2,1)S(1)}, u32[]{:S(2)}, u32[]{:S(2)}) async-start(bf16[16,18,3072]{2,1,0:T(8,128)(2,1)} %bitcast.63), calls=%async_computation.1 | async-start | bytes 4718592 | tf_op jit(solution)/shard_map/all_to_all | solution.py:94
  30.1 141.1 %all-gather.5.cloned.1.call-start = ((), (), s32[]{:S(2)}) async-start(), calls=%async_computation.4 | async-start | bytes 2228224 | tf_op jit(solution)/shard_map/all_gather | solution.py:87
  163.8 5.8 %copy-start.5 = (s32[128,1]{0,1:T(1,128)S(1)}, s32[128,1]{0,1:T(1,128)}, u32[]{:S(2)}) copy-start(s32[128,1]{0,1:T(1,128)} %param.20) | copy-start | bytes 1540
  163.8 5.8 %copy-start.2 = (bf16[128,3072]{1,0:T(8,128)(2,1)S(1)}, bf16[128,3072]{1,0:T(8,128)(2,1)}, u32[]{:S(2)}) copy-start(bf16[128,3072]{1,0:T(8,128)(2,1)} %param.14) | copy-start | bytes 2359300
  163.8 5.8 %copy-start.6 = (f32[3072]{0:T(1024)S(1)}, f32[3072]{0:T(1024)}, u32[]{:S(2)}) copy-start(f32[3072]{0:T(1024)} %param.18) | copy-start | bytes 36868
  163.8 57.3 %all-to-all-start.2 = ((bf16[16,18,3072]{2,1,0:T(8,128)(2,1)}), bf16[16,18,3072]{2,1,0:T(8,128)(2,1)}, u32[]{:S(2)}, u32[]{:S(2)}) async-start(bf16[16,18,3072]{2,1,0:T(8,128)(2,1)} %reshape.125), calls=%async_computation.2 | async-start | bytes 4718592 | tf_op jit(solution)/shard_map/all_to_all | solution.py:123
  168.3 2.8 %copy-start.4 = (bf16[128,3072]{1,0:T(8,128)(2,1)S(1)}, bf16[128,3072]{1,0:T(8,128)(2,1)}, u32[]{:S(2)}) copy-start(bf16[128,3072]{1,0:T(8,128)(2,1)} %param.15) | copy-start | bytes 2359300
  182.0 8.3 %copy-start.1 = (f32[4,2048,128,6]{2,1,3,0:T(8,128)}, f32[4,2048,128,6]{2,1,3,0:T(8,128)S(1)}, u32[]{:S(2)}) copy-start(f32[4,2048,128,6]{2,1,3,0:T(8,128)S(1)} %get-tuple-element.114) | copy-start | bytes 75497472 | tf_op jit(solution)/shard_map/cond
  223.3 1.2 copy-start.3
Sparse Core Ops, SparseCore 0:
  10.2 54.8 all-gather.2
  67.2 48.4 all-gather.4
where the time goes:
time: 234 us; the launch traced here: 233 us
  waiting for transfers between devices  76.8 us (33%)
  matrix products  59.8 us (26%)
  local copies, waits for them, and re-layouts  44.4 us (19%)
  other arithmetic  18.4 us (8%)
  starting transfers between devices  17.3 us (7%)
  between operations  15.5 us (7%)
    all_to_all x1, waiting for transfers between devices, body(): lax.all_to_all(send_rows, 'ctx', split_axis=0, concat_axis=0, tiled=True)  58.9 us
    dot_general x3, matrix products, expert_slice(): return jnp.dot(hidden, down_rows, preferred_element_type=jnp.float32)  23.7 us
    dot_general x3, matrix products, expert_slice(): lax.dot_general(rows, gate_rows, dims, preferred_element_type=jnp.float32)  17.4 us
    all_to_all x1, waiting for transfers between devices, body(): lax.all_to_all(returned, 'ctx', split_axis=0, concat_axis=0, tiled=True)  15.7 us
    cond x1, matrix products, body(): lax.cond(jnp.int32(0) > last_query, lambda: running, lambda: fold_block(r...  11.2 us
    gather x3, local copies, waits for them, and re-layouts, run_block(): rows = jnp.take(flat_rows, jnp.minimum(picked_slots, total - 1), axis=0)  10.6 us
    scatter x3, local copies, waits for them, and re-layouts, run_block(): return written.at[dest].set(result)  7.89 us
    all_to_all x1, starting transfers between devices, body(): lax.all_to_all(send_flags, 'ctx', split_axis=0, concat_axis=0, tiled=True)  6.55 us
  transfers between devices with their start and end apart: 5, of which 3 were waited for; matrix products, arithmetic and copies ran while one was open for 50% of the time, Pallas kernels for 0%

commit v1 on v0

v1 whole, which is shorter than its diff:
```python
import functools
import math

import jax
import jax.numpy as jnp
from jax import lax
from jax.experimental import pallas as pl
from jax.experimental.pallas import tpu as pltpu
from jax.sharding import PartitionSpec as P

HD = 128
E = 2
CAP = 18
MAIN = 16
Q = 4
MESH = pl.DeviceIdType.MESH
F32 = jnp.float32
BF16 = jnp.bfloat16
NT = (((1,), (1,)), ((), ()))


def iota(shape, dim):
    return lax.broadcasted_iota(jnp.int32, shape, dim)


def onehot(mask):
    return jnp.where(mask, 1.0, 0.0).astype(BF16)


def kernel(n, states, queries, keys, values, gain, router, routes, w_gate, w_up, w_down,
           attended, mixed, kv, x, x2, xb, part, hid, wg, wu, wd, r1, r2, r3, qs, m_sc, l_sc, acc,
           w_sem, loc_sem, kv_send, kv_recv, x_send, x_recv, r_send, r_recv, z_send, z_recv):
    rows, width = states.shape
    lines = n // Q
    per = lines // E
    kvw = keys.shape[1]
    heads = kvw // HD
    group = queries.shape[1] // kvw
    pack = width // 8
    wide = width + pack
    me = lax.axis_index("ctx")
    z = me // Q
    y = (me % Q) // 2
    c = me % 2
    ymate = z * Q + (1 - y) * 2 + c
    cmate = z * Q + y * 2 + (1 - c)

    def dev(zz, yy, cc):
        return zz * Q + yy * 2 + cc

    def slot(p):
        return ((p % 2) * 2 + (p % Q) // 2) * lines + p // Q

    def wcopy(i):
        src = (w_gate, w_up, w_down)[i]
        dst = (wg, wu, wd)[i]
        return pltpu.make_async_copy(src, dst, w_sem.at[i])

    def own_kv(i):
        src = (keys, values)[i]
        return pltpu.make_async_copy(
            src, kv.at[pl.ds(pl.multiple_of(me * rows, rows), rows), pl.ds(i * kvw, kvw)], loc_sem.at[i])

    own_kv(0).start()
    own_kv(1).start()
    for i in range(3):
        wcopy(i).start()

    barrier = pltpu.get_barrier_semaphore()
    for d in range(1, lines):
        pl.semaphore_signal(barrier, inc=1, device_id={"ctx": dev((z + d) % lines, y, c)}, device_id_type=MESH)
    for mate in (ymate, cmate):
        pl.semaphore_signal(barrier, inc=1, device_id={"ctx": mate}, device_id_type=MESH)

    def kv_block(p):
        return kv.at[pl.ds(pl.multiple_of(p * rows, rows), rows)]

    def kv_copy(kind, index, p, to):
        return pltpu.make_async_remote_copy(
            src_ref=kv_block(p), dst_ref=kv_block(p), send_sem=kv_send.at[kind, index], recv_sem=kv_recv.at[p],
            device_id={"ctx": to}, device_id_type=MESH)

    def x_block(p):
        return x.at[pl.ds(pl.multiple_of(slot(p) * MAIN, MAIN), MAIN)]

    def x_copy(kind, index, p, to):
        return pltpu.make_async_remote_copy(
            src_ref=x_block(p), dst_ref=x_block(p), send_sem=x_send.at[kind, index], recv_sem=x_recv.at[p],
            device_id={"ctx": to}, device_id_type=MESH)

    def x_line(zt):
        return pltpu.make_async_remote_copy(
            src_ref=xb.at[pl.ds((zt // per) * MAIN, MAIN)], dst_ref=x_block(me), send_sem=x_send.at[0, zt],
            recv_sem=x_recv.at[me], device_id={"ctx": dev(zt, y, c)}, device_id_type=MESH)

    st = states[...].astype(F32)
    meansq = jnp.mean(st * st, axis=-1, keepdims=True)
    normed = (st * lax.rsqrt(meansq + 1e-05) * gain[...]).astype(BF16)
    chosen = routes[...]
    member = chosen == iota((rows, HD), 1)
    before = onehot(iota((rows, rows), 1) < iota((rows, rows), 0))
    ahead = jnp.dot(before, onehot(member), preferred_element_type=F32)
    rank = jnp.sum(jnp.where(member, ahead, 0.0), axis=1, keepdims=True).astype(jnp.int32)
    lane = iota((rows, HD), 1)
    main_slot = jnp.where((chosen < E) & (rank < MAIN), chosen * MAIN + rank, -1)
    place = jnp.transpose(jnp.where(main_slot == lane, 1.0, 0.0)).astype(BF16)[: E * MAIN]
    xb[:, :width] = jnp.dot(place, normed, preferred_element_type=F32).astype(BF16)
    ext_slot = jnp.where((chosen < E) & (rank >= MAIN), chosen * MAIN + (rank - MAIN) * 8, -HD)
    ext = jnp.zeros((E * MAIN, pack), F32)
    for k in range(8):
        sel = jnp.transpose(jnp.where(ext_slot + k == lane, 1.0, 0.0)).astype(BF16)[: E * MAIN]
        ext += jnp.dot(sel, normed[:, k * pack:(k + 1) * pack], preferred_element_type=F32)
    xb[:, width:] = ext.astype(BF16)
    logits = jnp.dot(normed, router[...], preferred_element_type=F32)
    picked = jnp.sum(jnp.where(chosen == iota(logits.shape, 1), logits, 0.0), axis=1, keepdims=True)
    mixing = jax.nn.sigmoid(picked)

    x[pl.ds(pl.multiple_of(slot(me) * MAIN, MAIN), MAIN), :] = jnp.where(z < per, xb[:MAIN, :], xb[MAIN:, :])

    pl.semaphore_wait(barrier, lines + 1)

    for zt in range(lines):
        @pl.when(zt != z)
        def _(zt=zt):
            x_line(zt).start()

    def x_forward(d):
        zs = (z + d) % lines
        p = dev(zs, y, c)
        if d:
            x_copy(0, 0, p, me).wait_recv()
        x_copy(1, d, p, ymate).start()
        x_copy(2, d, p, cmate).start()

    def x_forward_y(d):
        zs = (z + d) % lines
        p = dev(zs, 1 - y, c)
        x_copy(1, d, p, ymate).wait_recv()
        x_copy(3, d, p, cmate).start()

    def x_wait(d):
        zs = (z + d) % lines
        x_copy(2, d, dev(zs, y, 1 - c), cmate).wait_recv()
        x_copy(3, d, dev(zs, 1 - y, 1 - c), cmate).wait_recv()

    def kv_line(d):
        return kv_copy(0, d, me, dev(z + d, y, c))

    def kv_forward(d):
        p = dev(z - d, y, c)

        @pl.when(z >= d)
        def _():
            if d:
                kv_copy(0, d, p, me).wait_recv()
            kv_copy(1, d, p, ymate).start()
            kv_copy(2, d, p, cmate).start()

    def kv_forward_y(d):
        p = dev(z - d, 1 - y, c)

        @pl.when(z >= d)
        def _():
            kv_copy(1, d, p, ymate).wait_recv()
            kv_copy(3, d, p, cmate).start()

    def kv_wait(d):
        @pl.when(z >= d)
        def _():
            kv_copy(2, d, dev(z - d, y, 1 - c), cmate).wait_recv()
            kv_copy(3, d, dev(z - d, 1 - y, 1 - c), cmate).wait_recv()

    x_forward(0)
    own_kv(0).wait()
    own_kv(1).wait()
    for d in range(1, lines):
        @pl.when(z + d < lines)
        def _(d=d):
            kv_line(d).start()
    kv_forward(0)

    for h in range(heads * group):
        qs[h * rows:(h + 1) * rows, :] = queries[:, h * HD:(h + 1) * HD]

    block = group * rows
    span = Q * rows
    scale = math.log2(math.e) / math.sqrt(HD)

    def attend(zs, masked):
        def head(h, carry):
            at = pl.ds(pl.multiple_of(h * block, block), block)
            keys_at = pl.ds(pl.multiple_of(zs * span, span), span)
            k = kv[keys_at, pl.ds(pl.multiple_of(h * HD, HD), HD)]
            v = kv[keys_at, pl.ds(pl.multiple_of(kvw + h * HD, HD), HD)]
            s = lax.dot_general(qs[at, :], k, NT, preferred_element_type=F32) * scale
            if masked:
                seen = iota((block, span), 1) <= (me % Q) * rows + iota((block, span), 0) % rows
                s = jnp.where(seen, s, -1e30)
            top = jnp.max(s, axis=-1, keepdims=True)
            if not masked:
                old = m_sc[at, :1]
                top = jnp.maximum(old, top)
            e = jnp.exp2(s - top)
            total = jnp.sum(e, axis=-1, keepdims=True)
            out = jnp.dot(e.astype(BF16), v, preferred_element_type=F32)
            if not masked:
                fade = jnp.exp2(old - top)
                total += fade * l_sc[at, :1]
                out += fade * acc[at, :]
            m_sc[at, :] = jnp.broadcast_to(top, (block, HD))
            l_sc[at, :] = jnp.broadcast_to(total, (block, HD))
            acc[at, :] = out
            return carry

        lax.fori_loop(0, heads, head, 0)

    for d in range(1, lines):
        x_forward(d)
    for d in range(lines):
        x_forward_y(d)
    kv_forward_y(0)
    for d in range(lines):
        x_wait(d)

    slots = n * MAIN
    over = 2 * n

    def unpick(k, shape, s_dim):
        j, i = iota(shape, 1 - s_dim), iota(shape, s_dim)
        return onehot((i // MAIN == j // 2) & (i % MAIN == (j % 2) * 8 + k))

    x2[:slots, :] = x[:, :width]
    for k in range(8):
        x2[slots:, k * pack:(k + 1) * pack] = jnp.dot(
            unpick(k, (over, slots), 1), x[:, width:], preferred_element_type=F32).astype(BF16)

    units = w_gate.shape[0]
    chunk = min(256, units)
    wcopy(0).wait()
    wcopy(1).wait()
    steps = units // chunk

    def gate_up(i, carry):
        at = pl.ds(pl.multiple_of(i * chunk, chunk), chunk)
        g = lax.dot_general(x2[...], wg[at, :], NT, preferred_element_type=F32)
        u = lax.dot_general(x2[...], wu[at, :], NT, preferred_element_type=F32)
        hid[:, at] = (g / (1.0 + jnp.exp(-g)) * u).astype(BF16)
        return carry

    lax.fori_loop(0, steps // 2, gate_up, 0)
    if lines > 1:
        kv_forward(1)
    lax.fori_loop(steps // 2, steps, gate_up, 0)
    if lines > 1:
        kv_forward_y(1)
    if lines > 2:
        kv_forward(2)
    wcopy(2).wait()

    part[:, width:] = jnp.zeros((slots, pack), BF16)

    def down(i, carry):
        at = pl.ds(pl.multiple_of(i * 2 * pack, 2 * pack), 2 * pack)
        o = jnp.dot(hid[...], wd[:, at], preferred_element_type=F32).astype(BF16)
        part[:, at] = o[:slots]
        for k in range(2):
            part[:, width:] += jnp.dot(
                unpick(2 * i + k, (slots, over), 0), o[slots:, k * pack:(k + 1) * pack],
                preferred_element_type=F32).astype(BF16)
        return carry

    lax.fori_loop(0, 4, down, 0)

    half, quart = slots // 2, slots // 4

    def core_swap():
        return pltpu.make_async_remote_copy(
            src_ref=part.at[pl.ds(pl.multiple_of((1 - c) * half, half), half)], dst_ref=r1,
            send_sem=r_send.at[0], recv_sem=r_recv.at[0], device_id={"ctx": cmate}, device_id_type=MESH)

    def y_swap():
        return pltpu.make_async_remote_copy(
            src_ref=part.at[pl.ds(pl.multiple_of((c * 2 + 1 - y) * quart, quart), quart)], dst_ref=r2,
            send_sem=r_send.at[1], recv_sem=r_recv.at[1], device_id={"ctx": ymate}, device_id_type=MESH)

    def line_back(zt, at):
        return pltpu.make_async_remote_copy(
            src_ref=part.at[pl.ds(pl.multiple_of((c * 2 + y) * quart + zt * MAIN, MAIN), MAIN)], dst_ref=r3.at[pl.ds(pl.multiple_of(at * MAIN, MAIN), MAIN)],
            send_sem=z_send.at[zt], recv_sem=z_recv.at[at], device_id={"ctx": dev(zt, y, c)}, device_id_type=MESH)

    core_swap().start()
    kv_wait(0)
    attend(z, True)
    for d in range(3, lines):
        kv_forward(d)
    for d in range(2, lines):
        kv_forward_y(d)

    core_swap().wait_recv()
    mine = pl.ds(pl.multiple_of(c * half, half), half)
    part[mine, :] = (part[mine, :].astype(F32) + r1[...].astype(F32)).astype(BF16)
    y_swap().start()
    if lines > 1:
        kv_wait(1)

        @pl.when(z >= 1)
        def _():
            attend(z - 1, False)

    y_swap().wait_recv()
    mine = pl.ds(pl.multiple_of((c * 2 + y) * quart, quart), quart)
    part[mine, :] = (part[mine, :].astype(F32) + r2[...].astype(F32)).astype(BF16)
    for zt in range(lines):
        @pl.when(zt != z)
        def _(zt=zt):
            line_back(zt, z).start()

        @pl.when(zt == z)
        def _(zt=zt):
            r3[zt * MAIN:(zt + 1) * MAIN, :] = part[pl.ds(pl.multiple_of((c * 2 + y) * quart + zt * MAIN, MAIN), MAIN), :]

    for d in range(2, lines):
        kv_wait(d)

    def far(d, carry):
        attend(z - d, False)
        return carry

    lax.fori_loop(2, z + 1, far, 0)

    def write(h, carry):
        at = pl.ds(pl.multiple_of(h * block, block), block)
        o = (acc[at, :] / l_sc[at, :]).astype(BF16)
        for g in range(group):
            attended[:, pl.ds(pl.multiple_of(h * block + g * HD, HD), HD)] = o[g * rows:(g + 1) * rows, :]
        return carry

    lax.fori_loop(0, heads, write, 0)

    for zs in range(lines):
        @pl.when(zs != z)
        def _(zs=zs):
            line_back(zs, zs).wait_recv()

    col = iota((rows, lines * MAIN), 1)
    owns = chosen == col // (per * MAIN)
    pick_main = onehot(owns & (rank == col % MAIN))
    for k in range(8):
        at = slice(k * pack, (k + 1) * pack)
        pick_ext = onehot(owns & (rank >= MAIN) & ((rank - MAIN) * 8 + k == col % MAIN))
        sums = jnp.dot(pick_main, r3[:, at], preferred_element_type=F32)
        sums += jnp.dot(pick_ext, r3[:, width:], preferred_element_type=F32)
        mixed[:, at] = (states[:, at].astype(F32) + mixing * sums).astype(BF16)

    core_swap().wait_send()
    y_swap().wait_send()
    for zt in range(lines):
        @pl.when(zt != z)
        def _(zt=zt):
            line_back(zt, z).wait_send()
            x_line(zt).wait_send()
    for d in range(lines):
        p = dev((z + d) % lines, y, c)
        x_copy(1, d, p, ymate).wait_send()
        x_copy(2, d, p, cmate).wait_send()
        x_copy(3, d, dev((z + d) % lines, 1 - y, c), cmate).wait_send()

        @pl.when(z >= d)
        def _(d=d):
            kv_copy(1, d, dev(z - d, y, c), ymate).wait_send()
            kv_copy(2, d, dev(z - d, y, c), cmate).wait_send()
            kv_copy(3, d, dev(z - d, 1 - y, c), cmate).wait_send()
        if d:
            @pl.when(z + d < lines)
            def _(d=d):
                kv_line(d).wait_send()


def solution(mesh):
    n = mesh.shape["ctx"]
    lines = n // Q

    def body(states, queries, keys, values, norm_gain, router, routes, w_gate, w_up, w_down):
        rows, width = states.shape
        kvw = keys.shape[1]
        units = w_gate.shape[0]
        qrows = rows * queries.shape[1] // HD
        slots = n * MAIN
        wide = width + width // 8
        vm = pl.BlockSpec(memory_space=pltpu.VMEM)
        hb = pl.BlockSpec(memory_space=pl.ANY)
        dma = pltpu.SemaphoreType.DMA
        return pl.pallas_call(
            functools.partial(kernel, n),
            out_shape=(jax.ShapeDtypeStruct(queries.shape, BF16), jax.ShapeDtypeStruct(states.shape, BF16)),
            in_specs=[vm, vm, hb, hb, vm, vm, vm, hb, hb, hb],
            out_specs=(vm, vm),
            scratch_shapes=[
                pltpu.VMEM((n * rows, 2 * kvw), BF16),
                pltpu.VMEM((slots, wide), BF16),
                pltpu.VMEM((slots + 2 * n, width), BF16),
                pltpu.VMEM((E * MAIN, wide), BF16),
                pltpu.VMEM((slots, wide), BF16),
                pltpu.VMEM((slots + 2 * n, units), BF16),
                pltpu.VMEM((units, width), BF16),
                pltpu.VMEM((units, width), BF16),
                pltpu.VMEM((units, width), BF16),
                pltpu.VMEM((slots // 2, wide), BF16),
                pltpu.VMEM((slots // 4, wide), BF16),
                pltpu.VMEM((lines * MAIN, wide), BF16),
                pltpu.VMEM((qrows, HD), BF16),
                pltpu.VMEM((qrows, HD), F32),
                pltpu.VMEM((qrows, HD), F32),
                pltpu.VMEM((qrows, HD), F32),
                dma((3,)),
                dma((2,)),
                dma((4, lines)),
                dma((n,)),
                dma((4, lines)),
                dma((n,)),
                dma((2,)),
                dma((2,)),
                dma((lines,)),
                dma((lines,)),
            ],
            compiler_params=pltpu.CompilerParams(
                collective_id=0, has_side_effects=True, vmem_limit_bytes=63 * 1024 * 1024),
        )(states, queries, keys, values, norm_gain.reshape(1, width), router, routes, w_gate, w_up, w_down)

    tokens = P(("groups", "ctx"), None)
    units = P("ctx", None)
    return jax.shard_map(
        body, mesh=mesh,
        in_specs=(tokens, tokens, tokens, tokens, P(), P(), tokens, units, units, units),
        out_specs=(tokens, tokens), check_vma=False)
```

time: 234 us -> 97.8 us (0.42)
  the two profiles are of different devices: /device:TPU:13 before, /device:TPU:24 now
where the time goes in v1:
time: 97.8 us; the launch traced here: 97.5 us
  Pallas kernels  89.4 us (91%)
  local copies, waits for them, and re-layouts  7.47 us (8%)
    pallas_call x1, Pallas kernels, body(): pl.pallas_call(functools.partial(kernel, n), out_shape=(jax.ShapeDtypeStr...  89.4 us
    unnamed x4, local copies, waits for them, and re-layouts  7.47 us

profile of v1, /device:TPU:24, one launch (start us, length us, event | category | flops | bytes accessed | tf_op | source)
XLA Modules:
  0.0 97.5 jit_solution(7962571529095820461)
XLA Ops:
  0.6 1.4 %copy.13.routes = s32[128,1]{1,0:T(8,128)} copy(s32[128,1]{0,1:T(1,128)} %param.16) | data formatting | bytes 1024 | tf_op args[6]
  2.0 2.0 %copy.12.router = bf16[3072,8]{1,0:T(8,128)(2,1)} copy(bf16[3072,8]{0,1:T(8,128)(2,1)} %param.15) | data formatting | bytes 98304 | tf_op args[5]
  4.0 89.4 %shard_map.113 = (bf16[128,3072]{1,0:T(8,128)(2,1)}, bf16[128,3072]{1,0:T(8,128)(2,1)}) custom-call(bf16[128,3072]{1,0:T(8,128)(2,1)} %states.1, bf16[128,3072]{1,0:T(8,128)(2,1)} %queries.1, bf16[128,512]{1,0:T(8,128)(2,1)} %keys.1, bf16[128,512]{1,0:T(8,128)(2,1)} %values.1, f32[1,3072]{1,0:T(1,128)} %bitcast.1, bf16[3072,8]{1,0:T(8,128)(2,1)} %copy.12.router, ...), custom_call_target="tpu_custom_call" | custom-call | tf_op jit(solution)/shard_map/pallas_call | solution.py:393
  93.4 2.1 %copy.16 = bf16[128,3072]{1,0:T(8,128)(2,1)} copy(bf16[128,3072]{1,0:T(8,128)(2,1)} %get-tuple-element.4) | data formatting | bytes 1572864
  95.5 2.1 %copy.17 = bf16[128,3072]{1,0:T(8,128)(2,1)} copy(bf16[128,3072]{1,0:T(8,128)(2,1)} %get-tuple-element.5) | data formatting | bytes 1572864

commit v2 on v1

--- a/solution.py
+++ b/solution.py
@@ -93,31 +93,66 @@
             src_ref=xb.at[pl.ds((zt // per) * MAIN, MAIN)], dst_ref=x_block(me), send_sem=x_send.at[0, zt],
             recv_sem=x_recv.at[me], device_id={"ctx": dev(zt, y, c)}, device_id_type=MESH)
 
+    def kv_line(d):
+        return kv_copy(0, d, me, dev(z + d, y, c))
+
+    def kv_forward(d):
+        p = dev(z - d, y, c)
+
+        @pl.when(z >= d)
+        def _():
+            if d:
+                kv_copy(0, d, p, me).wait_recv()
+            kv_copy(1, d, p, ymate).start()
+            kv_copy(2, d, p, cmate).start()
+
+    def kv_forward_y(d):
+        p = dev(z - d, 1 - y, c)
+
+        @pl.when(z >= d)
+        def _():
+            kv_copy(1, d, p, ymate).wait_recv()
+            kv_copy(3, d, p, cmate).start()
+
+    def kv_wait(d):
+        @pl.when(z >= d)
+        def _():
+            kv_copy(2, d, dev(z - d, y, 1 - c), cmate).wait_recv()
+            kv_copy(3, d, dev(z - d, 1 - y, 1 - c), cmate).wait_recv()
+
+    own_kv(0).wait()
+    own_kv(1).wait()
+    pl.semaphore_wait(barrier, lines + 1)
+    kv_forward(0)
+
     st = states[...].astype(F32)
     meansq = jnp.mean(st * st, axis=-1, keepdims=True)
     normed = (st * lax.rsqrt(meansq + 1e-05) * gain[...]).astype(BF16)
-    chosen = routes[...]
+    chosen = jnp.transpose(jnp.broadcast_to(routes[...].astype(F32), (HD, rows)))[:, :1].astype(jnp.int32)
     member = chosen == iota((rows, HD), 1)
     before = onehot(iota((rows, rows), 1) < iota((rows, rows), 0))
     ahead = jnp.dot(before, onehot(member), preferred_element_type=F32)
     rank = jnp.sum(jnp.where(member, ahead, 0.0), axis=1, keepdims=True).astype(jnp.int32)
-    lane = iota((rows, HD), 1)
+    down_rows = iota((E * MAIN, rows), 0)
+
+    def across(v):
+        return jnp.transpose(jnp.broadcast_to(v.astype(F32), (rows, HD)))[: E * MAIN].astype(jnp.int32)
+
     main_slot = jnp.where((chosen < E) & (rank < MAIN), chosen * MAIN + rank, -1)
-    place = jnp.transpose(jnp.where(main_slot == lane, 1.0, 0.0)).astype(BF16)[: E * MAIN]
+    place = onehot(across(main_slot) == down_rows)
     xb[:, :width] = jnp.dot(place, normed, preferred_element_type=F32).astype(BF16)
     ext_slot = jnp.where((chosen < E) & (rank >= MAIN), chosen * MAIN + (rank - MAIN) * 8, -HD)
+    ext_slot = across(ext_slot)
     ext = jnp.zeros((E * MAIN, pack), F32)
     for k in range(8):
-        sel = jnp.transpose(jnp.where(ext_slot + k == lane, 1.0, 0.0)).astype(BF16)[: E * MAIN]
+        sel = onehot(ext_slot + k == down_rows)
         ext += jnp.dot(sel, normed[:, k * pack:(k + 1) * pack], preferred_element_type=F32)
     xb[:, width:] = ext.astype(BF16)
-    logits = jnp.dot(normed, router[...], preferred_element_type=F32)
+    logits = lax.dot_general(normed, router[...], NT, preferred_element_type=F32)
     picked = jnp.sum(jnp.where(chosen == iota(logits.shape, 1), logits, 0.0), axis=1, keepdims=True)
     mixing = jax.nn.sigmoid(picked)
 
     x[pl.ds(pl.multiple_of(slot(me) * MAIN, MAIN), MAIN), :] = jnp.where(z < per, xb[:MAIN, :], xb[MAIN:, :])
-
-    pl.semaphore_wait(barrier, lines + 1)
 
     for zt in range(lines):
         @pl.when(zt != z)
@@ -143,42 +178,11 @@
         x_copy(2, d, dev(zs, y, 1 - c), cmate).wait_recv()
         x_copy(3, d, dev(zs, 1 - y, 1 - c), cmate).wait_recv()
 
-    def kv_line(d):
-        return kv_copy(0, d, me, dev(z + d, y, c))
-
-    def kv_forward(d):
-        p = dev(z - d, y, c)
-
-        @pl.when(z >= d)
-        def _():
-            if d:
-                kv_copy(0, d, p, me).wait_recv()
-            kv_copy(1, d, p, ymate).start()
-            kv_copy(2, d, p, cmate).start()
-
-    def kv_forward_y(d):
-        p = dev(z - d, 1 - y, c)
-
-        @pl.when(z >= d)
-        def _():
-            kv_copy(1, d, p, ymate).wait_recv()
-            kv_copy(3, d, p, cmate).start()
-
-    def kv_wait(d):
-        @pl.when(z >= d)
-        def _():
-            kv_copy(2, d, dev(z - d, y, 1 - c), cmate).wait_recv()
-            kv_copy(3, d, dev(z - d, 1 - y, 1 - c), cmate).wait_recv()
-
     x_forward(0)
-    own_kv(0).wait()
-    own_kv(1).wait()
     for d in range(1, lines):
         @pl.when(z + d < lines)
         def _(d=d):
             kv_line(d).start()
-    kv_forward(0)
-
     for h in range(heads * group):
         qs[h * rows:(h + 1) * rows, :] = queries[:, h * HD:(h + 1) * HD]
 
@@ -186,39 +190,47 @@
     span = Q * rows
     scale = math.log2(math.e) / math.sqrt(HD)
 
-    def attend(zs, masked):
+    tile = block // 2
+
+    def attend(zs, masked, first=0, last=heads):
         def head(h, carry):
-            at = pl.ds(pl.multiple_of(h * block, block), block)
             keys_at = pl.ds(pl.multiple_of(zs * span, span), span)
             k = kv[keys_at, pl.ds(pl.multiple_of(h * HD, HD), HD)]
             v = kv[keys_at, pl.ds(pl.multiple_of(kvw + h * HD, HD), HD)]
-            s = lax.dot_general(qs[at, :], k, NT, preferred_element_type=F32) * scale
-            if masked:
-                seen = iota((block, span), 1) <= (me % Q) * rows + iota((block, span), 0) % rows
-                s = jnp.where(seen, s, -1e30)
-            top = jnp.max(s, axis=-1, keepdims=True)
-            if not masked:
-                old = m_sc[at, :1]
-                top = jnp.maximum(old, top)
-            e = jnp.exp2(s - top)
-            total = jnp.sum(e, axis=-1, keepdims=True)
-            out = jnp.dot(e.astype(BF16), v, preferred_element_type=F32)
-            if not masked:
-                fade = jnp.exp2(old - top)
-                total += fade * l_sc[at, :1]
-                out += fade * acc[at, :]
-            m_sc[at, :] = jnp.broadcast_to(top, (block, HD))
-            l_sc[at, :] = jnp.broadcast_to(total, (block, HD))
-            acc[at, :] = out
+            both = jnp.concatenate([v, jnp.ones((span, HD), BF16)], axis=1)
+            for low in range(0, block, tile):
+                at = pl.ds(pl.multiple_of(h * block + low, tile), tile)
+                s = lax.dot_general(qs[at, :], k, NT, preferred_element_type=F32) * scale
+                if masked:
+                    seen = iota((tile, span), 1) <= (me % Q) * rows + iota((tile, span), 0) % rows
+                    s = jnp.where(seen, s, -1e30)
+                top = jnp.max(s, axis=-1, keepdims=True)
+                if not masked:
+                    old = m_sc[at, :1]
+                    top = jnp.maximum(old, top)
+                e = jnp.exp2(s - top).astype(BF16)
+                sums = jnp.dot(e, both, preferred_element_type=F32)
+                out, total = sums[:, :HD], sums[:, HD:]
+                if not masked:
+                    fade = jnp.exp2(old - top)
+                    total += fade * l_sc[at, :]
+                    out += fade * acc[at, :]
+                m_sc[at, :] = jnp.broadcast_to(top, (tile, HD))
+                l_sc[at, :] = total
+                acc[at, :] = out
             return carry
 
-        lax.fori_loop(0, heads, head, 0)
-
-    for d in range(1, lines):
-        x_forward(d)
+        lax.fori_loop(first, last, head, 0)
+
+    kv_forward_y(0)
+    kv_wait(0)
+    for h in range(heads):
+        attend(z, True, h, h + 1)
+        for d in range(1, lines):
+            if (d - 1) * heads // (lines - 1) == h:
+                x_forward(d)
     for d in range(lines):
         x_forward_y(d)
-    kv_forward_y(0)
     for d in range(lines):
         x_wait(d)
 
@@ -269,64 +281,88 @@
                 preferred_element_type=F32).astype(BF16)
         return carry
 
-    lax.fori_loop(0, 4, down, 0)
-
     half, quart = slots // 2, slots // 4
-
-    def core_swap():
+    sides = ((0, 4 * pack), (4 * pack, wide - 4 * pack))
+
+    def swap(src_at, dst, k, i, to):
+        cols = pl.ds(*sides[i])
         return pltpu.make_async_remote_copy(
-            src_ref=part.at[pl.ds(pl.multiple_of((1 - c) * half, half), half)], dst_ref=r1,
-            send_sem=r_send.at[0], recv_sem=r_recv.at[0], device_id={"ctx": cmate}, device_id_type=MESH)
-
-    def y_swap():
+            src_ref=part.at[src_at, cols], dst_ref=dst.at[:, cols], send_sem=r_send.at[k, i],
+            recv_sem=r_recv.at[k, i], device_id={"ctx": to}, device_id_type=MESH)
+
+    def core_swap(i):
+        return swap(pl.ds(pl.multiple_of((1 - c) * half, half), half), r1, 0, i, cmate)
+
+    def y_swap(i):
+        return swap(pl.ds(pl.multiple_of((c * 2 + 1 - y) * quart, quart), quart), r2, 1, i, ymate)
+
+    def own_rows(zt):
+        return pl.ds(pl.multiple_of((c * 2 + y) * quart + zt * MAIN, MAIN), MAIN)
+
+    def line_back(i, zt, at):
+        cols = pl.ds(*sides[i])
         return pltpu.make_async_remote_copy(
-            src_ref=part.at[pl.ds(pl.multiple_of((c * 2 + 1 - y) * quart, quart), quart)], dst_ref=r2,
-            send_sem=r_send.at[1], recv_sem=r_recv.at[1], device_id={"ctx": ymate}, device_id_type=MESH)
-
-    def line_back(zt, at):
-        return pltpu.make_async_remote_copy(
-            src_ref=part.at[pl.ds(pl.multiple_of((c * 2 + y) * quart + zt * MAIN, MAIN), MAIN)], dst_ref=r3.at[pl.ds(pl.multiple_of(at * MAIN, MAIN), MAIN)],
-            send_sem=z_send.at[zt], recv_sem=z_recv.at[at], device_id={"ctx": dev(zt, y, c)}, device_id_type=MESH)
-
-    core_swap().start()
-    kv_wait(0)
-    attend(z, True)
+            src_ref=part.at[own_rows(zt), cols],
+            dst_ref=r3.at[pl.ds(pl.multiple_of(at * MAIN, MAIN), MAIN), cols],
+            send_sem=z_send.at[i, zt], recv_sem=z_recv.at[i, at], device_id={"ctx": dev(zt, y, c)},
+            device_id_type=MESH)
+
+    def add(at, other, i):
+        cols = pl.ds(*sides[i])
+        part[at, cols] = (part[at, cols].astype(F32) + other[:, cols].astype(F32)).astype(BF16)
+
+    def after_core(i):
+        core_swap(i).wait_recv()
+        add(pl.ds(pl.multiple_of(c * half, half), half), r1, i)
+        y_swap(i).start()
+
+    def after_y(i):
+        y_swap(i).wait_recv()
+        add(pl.ds(pl.multiple_of((c * 2 + y) * quart, quart), quart), r2, i)
+        cols = pl.ds(*sides[i])
+        for zt in range(lines):
+            @pl.when(zt != z)
+            def _(zt=zt):
+                line_back(i, zt, z).start()
+
+            @pl.when(zt == z)
+            def _(zt=zt):
+                r3[zt * MAIN:(zt + 1) * MAIN, cols] = part[own_rows(zt), cols]
+
+    def attend_back(d, first, last):
+        if d < lines:
+            @pl.when(z >= d)
+            def _():
+                attend(z - d, False, first, last)
+
+    lax.fori_loop(0, 2, down, 0)
+    core_swap(0).start()
+    lax.fori_loop(2, 4, down, 0)
+    core_swap(1).start()
     for d in range(3, lines):
         kv_forward(d)
     for d in range(2, lines):
         kv_forward_y(d)
-
-    core_swap().wait_recv()
-    mine = pl.ds(pl.multiple_of(c * half, half), half)
-    part[mine, :] = (part[mine, :].astype(F32) + r1[...].astype(F32)).astype(BF16)
-    y_swap().start()
+    after_core(0)
     if lines > 1:
         kv_wait(1)
-
-        @pl.when(z >= 1)
-        def _():
-            attend(z - 1, False)
-
-    y_swap().wait_recv()
-    mine = pl.ds(pl.multiple_of((c * 2 + y) * quart, quart), quart)
-    part[mine, :] = (part[mine, :].astype(F32) + r2[...].astype(F32)).astype(BF16)
-    for zt in range(lines):
-        @pl.when(zt != z)
-        def _(zt=zt):
-            line_back(zt, z).start()
-
-        @pl.when(zt == z)
-        def _(zt=zt):
-            r3[zt * MAIN:(zt + 1) * MAIN, :] = part[pl.ds(pl.multiple_of((c * 2 + y) * quart + zt * MAIN, MAIN), MAIN), :]
-
-    for d in range(2, lines):
+    attend_back(1, 0, heads // 2)
+    after_core(1)
+    attend_back(1, heads // 2, heads)
+    after_y(0)
+    if lines > 2:
+        kv_wait(2)
+    attend_back(2, 0, heads // 2)
+    after_y(1)
+    attend_back(2, heads // 2, heads)
+    for d in range(3, lines):
         kv_wait(d)
 
     def far(d, carry):
         attend(z - d, False)
         return carry
 
-    lax.fori_loop(2, z + 1, far, 0)
+    lax.fori_loop(3, z + 1, far, 0)
 
     def write(h, carry):
         at = pl.ds(pl.multiple_of(h * block, block), block)
@@ -340,7 +376,8 @@
     for zs in range(lines):
         @pl.when(zs != z)
         def _(zs=zs):
-            line_back(zs, zs).wait_recv()
+            line_back(0, zs, zs).wait_recv()
+            line_back(1, zs, zs).wait_recv()
 
     col = iota((rows, lines * MAIN), 1)
     owns = chosen == col // (per * MAIN)
@@ -352,12 +389,14 @@
         sums += jnp.dot(pick_ext, r3[:, width:], preferred_element_type=F32)
         mixed[:, at] = (states[:, at].astype(F32) + mixing * sums).astype(BF16)
 
-    core_swap().wait_send()
-    y_swap().wait_send()
+    for i in range(2):
+        core_swap(i).wait_send()
+        y_swap(i).wait_send()
     for zt in range(lines):
         @pl.when(zt != z)
         def _(zt=zt):
-            line_back(zt, z).wait_send()
+            line_back(0, zt, z).wait_send()
+            line_back(1, zt, z).wait_send()
             x_line(zt).wait_send()
     for d in range(lines):
         p = dev((z + d) % lines, y, c)
@@ -418,14 +457,14 @@
                 dma((n,)),
                 dma((4, lines)),
                 dma((n,)),
-                dma((2,)),
-                dma((2,)),
-                dma((lines,)),
-                dma((lines,)),
+                dma((2, 2)),
+                dma((2, 2)),
+                dma((2, lines)),
+                dma((2, lines)),
             ],
             compiler_params=pltpu.CompilerParams(
                 collective_id=0, has_side_effects=True, vmem_limit_bytes=63 * 1024 * 1024),
-        )(states, queries, keys, values, norm_gain.reshape(1, width), router, routes, w_gate, w_up, w_down)
+        )(states, queries, keys, values, norm_gain.reshape(1, width), router.T, routes.T, w_gate, w_up, w_down)
 
     tokens = P(("groups", "ctx"), None)
     units = P("ctx", None)

time: 97.8 us -> 78.5 us (0.80)
  Pallas kernels: 89.4 us -> 73.5 us
  local copies, waits for them, and re-layouts: 7.47 us -> 4.13 us
    pallas_call x1, Pallas kernels: 89.4 us -> 73.5 us  [body(): pl.pallas_call(functools.partial(kernel, n), out_shape=(jax.ShapeDtypeStr...]
    unnamed x4 -> x2, local copies, waits for them, and re-layouts: 7.47 us -> 4.13 us
where the time goes in v2:
time: 78.5 us; the launch traced here: 78.3 us
  Pallas kernels  73.5 us (94%)
  local copies, waits for them, and re-layouts  4.13 us (5%)
    pallas_call x1, Pallas kernels, body(): pl.pallas_call(functools.partial(kernel, n), out_shape=(jax.ShapeDtypeStr...  73.5 us
    unnamed x2, local copies, waits for them, and re-layouts  4.13 us

profile of v2, /device:TPU:24, one launch (start us, length us, event | category | flops | bytes accessed | tf_op | source)
XLA Modules:
  0.0 78.3 jit_solution(800739011879190196)
XLA Ops:
  0.6 73.5 %shard_map.113 = (bf16[128,3072]{1,0:T(8,128)(2,1)}, bf16[128,3072]{1,0:T(8,128)(2,1)}) custom-call(bf16[128,3072]{1,0:T(8,128)(2,1)} %states.1, bf16[128,3072]{1,0:T(8,128)(2,1)} %queries.1, bf16[128,512]{1,0:T(8,128)(2,1)} %keys.1, bf16[128,512]{1,0:T(8,128)(2,1)} %values.1, f32[1,3072]{1,0:T(1,128)} %bitcast.4, bf16[8,3072]{1,0:T(8,128)(2,1)} %bitcast.3, ...), custom_call_target="tpu_custom_call" | custom-call | tf_op jit(solution)/shard_map/pallas_call | solution.py:432
  74.1 2.1 %copy.14 = bf16[128,3072]{1,0:T(8,128)(2,1)} copy(bf16[128,3072]{1,0:T(8,128)(2,1)} %get-tuple-element.4) | data formatting | bytes 1572864
  76.2 2.1 %copy.15 = bf16[128,3072]{1,0:T(8,128)(2,1)} copy(bf16[128,3072]{1,0:T(8,128)(2,1)} %get-tuple-element.5) | data formatting | bytes 1572864

commit v3 on v2

--- a/solution.py
+++ b/solution.py
@@ -94,7 +94,7 @@
             recv_sem=x_recv.at[me], device_id={"ctx": dev(zt, y, c)}, device_id_type=MESH)
 
     def kv_line(d):
-        return kv_copy(0, d, me, dev(z + d, y, c))
+        return kv_copy(0, d, dev(z - d + 1, y, c), dev(z + 1, y, c))
 
     def kv_forward(d):
         p = dev(z - d, y, c)
@@ -103,6 +103,10 @@
         def _():
             if d:
                 kv_copy(0, d, p, me).wait_recv()
+                if d + 1 < lines:
+                    @pl.when(z + 1 < lines)
+                    def _():
+                        kv_line(d + 1).start()
             kv_copy(1, d, p, ymate).start()
             kv_copy(2, d, p, cmate).start()
 
@@ -179,10 +183,10 @@
         x_copy(3, d, dev(zs, 1 - y, 1 - c), cmate).wait_recv()
 
     x_forward(0)
-    for d in range(1, lines):
-        @pl.when(z + d < lines)
-        def _(d=d):
-            kv_line(d).start()
+    if lines > 1:
+        @pl.when(z + 1 < lines)
+        def _():
+            kv_line(1).start()
     for h in range(heads * group):
         qs[h * rows:(h + 1) * rows, :] = queries[:, h * HD:(h + 1) * HD]
 
@@ -224,13 +228,12 @@
 
     kv_forward_y(0)
     kv_wait(0)
-    for h in range(heads):
-        attend(z, True, h, h + 1)
-        for d in range(1, lines):
-            if (d - 1) * heads // (lines - 1) == h:
-                x_forward(d)
-    for d in range(lines):
-        x_forward_y(d)
+    attend(z, True, 0, heads // 2)
+    for d in range(1, lines):
+        x_forward(d)
+        x_forward_y(d - 1)
+    x_forward_y(lines - 1)
+    attend(z, True, heads // 2, heads)
     for d in range(lines):
         x_wait(d)
 
@@ -410,7 +413,7 @@
             kv_copy(2, d, dev(z - d, y, c), cmate).wait_send()
             kv_copy(3, d, dev(z - d, 1 - y, c), cmate).wait_send()
         if d:
-            @pl.when(z + d < lines)
+            @pl.when((z >= d - 1) & (z + 1 < lines))
             def _(d=d):
                 kv_line(d).wait_send()
 

time: 78.5 us -> 76.6 us (0.976)
  Pallas kernels: 73.5 us -> 71.6 us
    pallas_call x1, Pallas kernels: 73.5 us -> 71.6 us  [body(): pl.pallas_call(functools.partial(kernel, n), out_shape=(jax.ShapeDtypeStr...]
where the time goes in v3:
time: 76.6 us; the launch traced here: 76.4 us
  Pallas kernels  71.6 us (93%)
  local copies, waits for them, and re-layouts  4.13 us (5%)
    pallas_call x1, Pallas kernels, body(): pl.pallas_call(functools.partial(kernel, n), out_shape=(jax.ShapeDtypeStr...  71.6 us
    unnamed x2, local copies, waits for them, and re-layouts  4.13 us

profile of v3, /device:TPU:24, one launch (start us, length us, event | category | flops | bytes accessed | tf_op | source)
XLA Modules:
  0.0 76.4 jit_solution(13023214110328621123)
XLA Ops:
  0.6 71.6 %shard_map.113 = (bf16[128,3072]{1,0:T(8,128)(2,1)}, bf16[128,3072]{1,0:T(8,128)(2,1)}) custom-call(bf16[128,3072]{1,0:T(8,128)(2,1)} %states.1, bf16[128,3072]{1,0:T(8,128)(2,1)} %queries.1, bf16[128,512]{1,0:T(8,128)(2,1)} %keys.1, bf16[128,512]{1,0:T(8,128)(2,1)} %values.1, f32[1,3072]{1,0:T(1,128)} %bitcast.4, bf16[8,3072]{1,0:T(8,128)(2,1)} %bitcast.3, ...), custom_call_target="tpu_custom_call" | custom-call | tf_op jit(solution)/shard_map/pallas_call | solution.py:435
  72.2 2.1 %copy.14 = bf16[128,3072]{1,0:T(8,128)(2,1)} copy(bf16[128,3072]{1,0:T(8,128)(2,1)} %get-tuple-element.4) | data formatting | bytes 1572864
  74.3 2.1 %copy.15 = bf16[128,3072]{1,0:T(8,128)(2,1)} copy(bf16[128,3072]{1,0:T(8,128)(2,1)} %get-tuple-element.5) | data formatting | bytes 1572864
